TPU v7x, 32 devices: a whole 2x2x4 slice. The times are simulated.
32 devices in a mesh: grp: 2 (over y), chan: 4 (over z), day: 2 (over x), seg: 2 (over core).
Axes of the slice: x: 2, y: 2, z: 4, core: 2. Of those that a mesh axis runs over, the one named last changes fastest.
Arguments:
- records: bfloat16 [4, 4, 512, 2048], P('day', 'seg', ('grp', 'chan')), parts along dimension 2, may hold values from -30 to 30
- visits: int32 [3, 2, 512], P(None, None, ('grp', 'chan')), parts along dimension 2, may hold values from 0 to 63
Outputs:
- correlation: bfloat16 [256, 3, 2, 512], P(('day', 'seg'), None, None, ('grp', 'chan')), parts along dimension 3
There are 2 independent parts, one for each index of `grp`. A program takes and returns all parts, laid end to end along the dimension named above; each array names one. Nothing has to cross between parts.
All inputs are finite; a program needn't handle non-finite values.
Results may differ from a plain program's by a relative error of at most 0.0068.
Values may be sent and summed in bfloat16 or wider, within the bound.
A program may use at most 64 MiB of HBM per device.

v0:
```python
import math

import jax
import jax.numpy as jnp
from jax import lax
from jax.sharding import PartitionSpec as P

NS = 2048
FREQS = 512
BAND = 64
LAGS = 256
SEGS = 4


def shifted(block, axis, distance):
    devices = range(lax.axis_size(axis))
    route = [((i - distance) % len(devices), i) for i in devices]
    return lax.ppermute(block, axis, route)


def forward_table():
    sample_index = lax.broadcasted_iota(jnp.int32, (NS, FREQS), 0)
    freq_index = lax.broadcasted_iota(jnp.int32, (NS, FREQS), 1)
    turns = (sample_index * freq_index % NS).astype(jnp.float32) * (2.0 * math.pi / NS)
    return jnp.concatenate([jnp.cos(turns), -jnp.sin(turns)], 1).astype(jnp.bfloat16)


def inverse_table():
    lag_index = lax.broadcasted_iota(jnp.int32, (LAGS, FREQS), 0) - LAGS // 2
    freq_index = lax.broadcasted_iota(jnp.int32, (LAGS, FREQS), 1)
    turns = (lag_index * freq_index % NS).astype(jnp.float32) * (2.0 * math.pi / NS)
    return jnp.concatenate([jnp.cos(turns), -jnp.sin(turns)], 1).astype(jnp.bfloat16)


def whiten(spectra):
    row_total = spectra.shape[0]
    real_part = spectra[:, :FREQS]
    imag_part = spectra[:, FREQS:]
    band_power = (
        jnp.mean(
            (real_part * real_part + imag_part * imag_part).reshape(row_total, FREQS // BAND, BAND),
            axis=-1,
        )
        * 0.5
    )
    factor = jnp.repeat(lax.rsqrt(band_power + 1e-06), BAND, axis=1)
    return jnp.concatenate([real_part * factor, imag_part * factor], 1).astype(jnp.bfloat16)


def pair_spectrum(own_block, held_block, picked):
    source_rows = jnp.take(held_block, picked, axis=1)
    own_real = own_block[:, None, :, :FREQS].astype(jnp.float32)
    own_imag = own_block[:, None, :, FREQS:].astype(jnp.float32)
    other_real = source_rows[..., :FREQS].astype(jnp.float32)
    other_imag = source_rows[..., FREQS:].astype(jnp.float32)
    real_sum = jnp.sum(own_real * other_real + own_imag * other_imag, axis=0)
    imag_sum = jnp.sum(own_real * other_imag - own_imag * other_real, axis=0)
    return jnp.concatenate([real_sum, imag_sum], -1).astype(jnp.bfloat16)


def lag_terms(flat_rows, table_rows):
    return lax.dot_general(
        table_rows, flat_rows, (((1,), (1,)), ((), ())), preferred_element_type=jnp.float32
    )


def local(records, visits):
    day_local = records.shape[0]
    seg_local = records.shape[1]
    chan_block = records.shape[2]
    spectra = jnp.dot(
        records.reshape(day_local * seg_local * chan_block, NS),
        forward_table(),
        preferred_element_type=jnp.float32,
    )
    whitened = whiten(spectra).reshape(day_local * seg_local, chan_block, 2 * FREQS)
    inverse = inverse_table()
    visit_count = visits.shape[0]
    picks = visits.shape[1]
    reach_blocks = lax.axis_size("chan") // 4
    lag_share = LAGS // (lax.axis_size("day") * lax.axis_size("seg"))

    def cross_spectrum(held_block, visit):
        picked = lax.dynamic_index_in_dim(visits, visit, 0, keepdims=False)
        return pair_spectrum(whitened, held_block, picked)

    def record_visit(stored, visit, cross_spec):
        updated = lax.dynamic_update_index_in_dim(stored, cross_spec, visit, 0)
        return updated

    stored = jnp.zeros((visit_count, picks, chan_block, 2 * FREQS), jnp.bfloat16)
    stored = record_visit(stored, reach_blocks, cross_spectrum(whitened, reach_blocks))

    def both_ways(offset, carry):
        upper, lower, stored_in = carry
        upper = shifted(upper, "chan", -1)
        lower = shifted(lower, "chan", 1)
        stored_in = record_visit(
            stored_in, reach_blocks - offset, cross_spectrum(upper, reach_blocks - offset)
        )
        stored_in = record_visit(
            stored_in, reach_blocks + offset, cross_spectrum(lower, reach_blocks + offset)
        )
        return (upper, lower, stored_in)

    carried = lax.fori_loop(1, reach_blocks + 1, both_ways, (whitened, whitened, stored))
    stored = carried[2]
    all_rows = stored.reshape(-1, 2 * FREQS)
    total = lax.psum_scatter(
        lag_terms(all_rows, inverse), ("day", "seg"), scatter_dimension=0, tiled=True
    ).reshape(lag_share, visit_count, picks, chan_block)
    days_all = day_local * lax.axis_size("day")
    scale_factor = 1.0 / math.sqrt(FREQS * days_all * SEGS)
    return (total * scale_factor).astype(jnp.bfloat16)


def solution(mesh):
    in_specs = (P("day", "seg", ("grp", "chan"), None), P(None, None, ("grp", "chan")))
    out_specs = P(("day", "seg"), None, None, ("grp", "chan"))
    return jax.shard_map(local, mesh=mesh, in_specs=in_specs, out_specs=out_specs, check_vma=False)
```

profile of v0, /device:TPU:0, one launch (start us, length us, event | category | flops | bytes accessed | tf_op | source)
XLA Modules:
  0.0 104.7 jit_solution(11911600990179981462)
XLA Ops:
  6.5 0.0 copy-start
  6.5 0.0 reduce-scatter.2.cloned.1.call-start
  6.5 17.1 %negate_convert_fusion = (bf16[2048,512]{1,0:T(8,128)(2,1)S(1)}, bf16[2048,512]{1,0:T(8,128)(2,1)S(1)}) fusion(), kind=kLoop, calls=%fused_computation.13 | loop fusion | flops 17825792 | bytes 4194304 | tf_op jit(solution)/shard_map/convert.17
  23.7 0.0 copy-done
  23.7 1.3 %fusion.11 = f32[256,1024]{1,0:T(8,128)S(1)} fusion(bf16[256,2048]{1,0:T(8,128)(2,1)S(1)} %bitcast.50, bf16[2048,512]{1,0:T(8,128)(2,1)S(1)} %get-tuple-element.47, bf16[2048,512]{1,0:T(8,128)(2,1)S(1)} %get-tuple-element.48), kind=kOutput, calls=%fused_computation.21 | convolution fusion | flops 1082130432 | bytes 6291456 | tf_op jit(solution)/shard_map/dot_general | solution.py:71
  24.9 0.1 multiply_add_fusion
  25.0 0.2 copy.3
  25.4 0.0 copy-start.6
  25.4 0.2 copy.4
  25.6 0.2 multiply_convert_fusion.1
  25.8 0.0 copy-start.1
  25.8 0.9 copy_dynamic-update-slice_fusion.1
  26.7 0.9 copy_dynamic-update-slice_fusion
  27.7 3.0 %collective-permute-start.1 = (bf16[4,64,1024]{2,0,1:T(4,128)(2,1)}, bf16[4,64,1024]{2,0,1:T(4,128)(2,1)}, u32[]{:S(2)}, u32[]{:S(2)}) collective-permute-start(bf16[4,64,1024]{2,0,1:T(4,128)(2,1)} %copy_dynamic-update-slice_fusion), channel_id=1, source_target_pairs={{12,0},{0,4},{4,8},{8,12},{13,1},{1,5},{5,9},{9,13},{14,2},{2,6},{... | collective-permute-start | bytes 1572872 | tf_op jit(solution)/shard_map/while/body/eval_jaxpr/ppermute | solution.py:18
  30.7 2.0 %collective-permute-start = (bf16[4,64,1024]{2,0,1:T(4,128)(2,1)}, bf16[4,64,1024]{2,0,1:T(4,128)(2,1)}, u32[]{:S(2)}, u32[]{:S(2)}) collective-permute-start(bf16[4,64,1024]{2,0,1:T(4,128)(2,1)} %copy_dynamic-update-slice_fusion), channel_id=1, source_target_pairs={{4,0},{8,4},{12,8},{0,12},{5,1},{9,5},{13,9},{1,13},{6,2},{10,6},{... | collective-permute-start | bytes 1572872 | tf_op jit(solution)/shard_map/while/body/eval_jaxpr/ppermute | solution.py:18
  32.7 0.0 copy-done.6
  32.7 0.1 reshape.165
  32.8 0.1 reshape.161
  32.9 0.1 reshape.157
  33.0 0.0 copy-done.1
  33.0 2.5 %gather_fusion = bf16[128,4,1024]{2,1,0:T(4,128)(2,1)S(1)} fusion(bf16[4,64,1024]{2,0,1:T(4,128)(2,1)} %copy_dynamic-update-slice_fusion, s32[1024]{0:T(1024)S(1)} %pad_clamp_fusion.2), kind=kCustom, calls=%fused_computation.clone | custom fusion | bytes 2097664 | tf_op jit(solution)/shard_map/jit(_take)/gather | solution.py:51
  35.5 0.0 copy-start.2
  35.5 0.6 select_bitcast_fusion.2
  36.1 0.3 copy-done.2
  36.4 1.0 copy.5
  37.4 1.0 copy.9
  38.5 3.1 %cosine_convert_fusion.1 = (bf16[256,512]{1,0:T(8,128)(2,1)S(1)}, bf16[256,512]{1,0:T(8,128)(2,1)}) fusion(s32[256]{0:T(256)S(1)} %iota_add_fusion), kind=kLoop, calls=%fused_computation.67 | loop fusion | flops 2228224 | bytes 525312 | tf_op jit(solution)/shard_map/convert.18
  41.5 4.3 %collective-permute-done.1 = bf16[4,64,1024]{2,0,1:T(4,128)(2,1)} collective-permute-done((bf16[4,64,1024]{2,0,1:T(4,128)(2,1)}, bf16[4,64,1024]{2,0,1:T(4,128)(2,1)}, u32[]{:S(2)}, u32[]{:S(2)}) %collective-permute-start.1) | collective-permute-done | bytes 524320 | tf_op jit(solution)/shard_map/while/body/eval_jaxpr/ppermute | solution.py:18
  45.8 3.4 %gather_fusion.2 = bf16[128,4,1024]{2,1,0:T(4,128)(2,1)} fusion(bf16[4,64,1024]{2,0,1:T(4,128)(2,1)} %collective-permute-done.1, s32[1024]{0:T(1024)S(1)} %pad_clamp_fusion), kind=kCustom, calls=%fused_computation.2.clone | custom fusion | bytes 2097664 | tf_op jit(solution)/shard_map/while/body/eval_jaxpr/jit(_take)/gather | solution.py:51
  49.2 1.8 %select_bitcast_fusion = bf16[4,2,64,1024]{3,0,2,1:T(4,128)(2,1)S(1)} fusion(bf16[2,64,4,1024]{3,2,1,0:T(4,128)(2,1)} %bitcast.52, pred[2,64]{1,0:T(4,128)(4,1)S(1)} %get-tuple-element.40), kind=kLoop, calls=%fused_computation.48 | loop fusion | flops 524288 | bytes 2097280 | tf_op jit(solution)/shard_map/while/body/eval_jaxpr/jit(_take)/select_n | solution.py:51
  51.0 4.6 %collective-permute-done = bf16[4,64,1024]{2,0,1:T(4,128)(2,1)} collective-permute-done((bf16[4,64,1024]{2,0,1:T(4,128)(2,1)}, bf16[4,64,1024]{2,0,1:T(4,128)(2,1)}, u32[]{:S(2)}, u32[]{:S(2)}) %collective-permute-start) | collective-permute-done | bytes 524320 | tf_op jit(solution)/shard_map/while/body/eval_jaxpr/ppermute | solution.py:18
  55.6 3.4 %gather_fusion.1 = bf16[128,4,1024]{2,1,0:T(4,128)(2,1)} fusion(bf16[4,64,1024]{2,0,1:T(4,128)(2,1)} %collective-permute-done, s32[1024]{0:T(1024)S(1)} %pad_clamp_fusion.1), kind=kCustom, calls=%fused_computation.1.clone | custom fusion | bytes 2097664 | tf_op jit(solution)/shard_map/while/body/eval_jaxpr/jit(_take)/gather | solution.py:51
  59.0 0.0 copy-start.3
  59.0 0.0 copy-start.4
  59.0 1.9 %select_bitcast_fusion.1 = bf16[4,2,64,1024]{3,0,2,1:T(4,128)(2,1)S(1)} fusion(bf16[2,64,4,1024]{3,2,1,0:T(4,128)(2,1)} %bitcast.51, pred[2,64]{1,0:T(4,128)(4,1)S(1)} %get-tuple-element.41), kind=kLoop, calls=%fused_computation.49 | loop fusion | flops 524288 | bytes 2097280 | tf_op jit(solution)/shard_map/while/body/eval_jaxpr/jit(_take)/select_n | solution.py:51
  60.9 0.0 copy-done.3
  60.9 0.0 copy-done.4
  60.9 6.9 %fusion.25 = (bf16[2,64,512]{2,1,0:T(8,128)(2,1)S(1)}, bf16[2,64,512]{2,1,0:T(8,128)(2,1)S(1)}, bf16[2,64,512]{2,1,0:T(8,128)(2,1)S(1)}, bf16[2,64,512]{2,1,0:T(...) fusion(f32[4,64,512]{2,0,1:T(4,128)S(1)} %copy-done.4, f32[4,64,512]{2,0,1:T(4,128)S(1)} %copy-done.3, ...), kind=kLoop, calls=%fused_computation.45 | loop fusion | flops 7471104 | bytes 4980736 | tf_op jit(solution)/shard_map/while/body/eval_jaxpr/reduce_sum | solution.py:56
  67.8 0.0 copy-start.5
  67.9 0.1 fusion.28
  68.0 0.8 copy-done.5
  68.8 1.2 %fusion.32 = f32[256,384]{1,0:T(8,128)} fusion(bf16[384,1024]{1,0:T(8,128)(2,1)S(1)} %bitcast.59, bf16[256,512]{1,0:T(8,128)(2,1)S(1)} %copy-done.5, bf16[256,512]{1,0:T(8,128)(2,1)S(1)} %get-tuple-element.45), kind=kOutput, calls=%fused_computation.58 | convolution fusion | flops 202375168 | bytes 1703936 | tf_op jit(solution)/shard_map/dot_general | solution.py:62
  70.0 0.0 reduce-scatter.2.cloned.1.call-update
  70.0 26.1 %reduce-scatter.2.cloned.1.call-done = f32[64,384]{1,0:T(8,128)} async-done(((f32[256,384]{1,0:T(8,128)}), f32[64,384]{1,0:T(8,128)}) %reduce-scatter.2.cloned.1.call-update) | async-done | bytes 98320 | tf_op jit(solution)/shard_map/reduce_scatter | solution.py:109
  96.2 0.9 multiply_convert_fusion.2
  97.1 0.8 convert_element_type.93
  (11 shorter events, 0.2 us)
Async XLA Ops:
  6.5 17.1 %copy-start = (bf16[2,2,64,2048]{3,2,1,0:T(8,128)(2,1)S(1)}, bf16[2,2,64,2048]{3,2,1,0:T(8,128)(2,1)}, u32[]{:S(2)}) copy-start(bf16[2,2,64,2048]{3,2,1,0:T(8,128)(2,1)} %param.4) | copy-start | bytes 3145732
  6.5 89.6 %reduce-scatter.2.cloned.1.call-start = ((), (), s32[]{:S(2)}) async-start(), calls=%async_computation.1 | async-start | bytes 491520 | tf_op jit(solution)/shard_map/reduce_scatter | solution.py:109
  25.4 7.4 %copy-start.6 = (s32[3,2,64]{2,1,0:T(2,128)S(1)}, s32[3,2,64]{2,1,0:T(2,128)}, u32[]{:S(2)}) copy-start(s32[3,2,64]{2,1,0:T(2,128)} %param.5) | copy-start | bytes 4612
  25.8 7.2 %copy-start.1 = (bf16[256,512]{1,0:T(8,128)(2,1)}, bf16[256,512]{1,0:T(8,128)(2,1)S(1)}, u32[]{:S(2)}) copy-start(bf16[256,512]{1,0:T(8,128)(2,1)S(1)} %get-tuple-element.37) | copy-start | bytes 786436
  27.7 18.2 %collective-permute-start.1 = (bf16[4,64,1024]{2,0,1:T(4,128)(2,1)}, bf16[4,64,1024]{2,0,1:T(4,128)(2,1)}, u32[]{:S(2)}, u32[]{:S(2)}) collective-permute-start(bf16[4,64,1024]{2,0,1:T(4,128)(2,1)} %copy_dynamic-update-slice_fusion), channel_id=1, source_target_pairs={{12,0},{0,4},{4,8},{8,12},{13,1},{1,5},{5,9},{9,13},{14,2},{2,6},{... | collective-permute-start | bytes 1572872 | tf_op jit(solution)/shard_map/while/body/eval_jaxpr/ppermute | solution.py:18
  30.7 24.9 %collective-permute-start = (bf16[4,64,1024]{2,0,1:T(4,128)(2,1)}, bf16[4,64,1024]{2,0,1:T(4,128)(2,1)}, u32[]{:S(2)}, u32[]{:S(2)}) collective-permute-start(bf16[4,64,1024]{2,0,1:T(4,128)(2,1)} %copy_dynamic-update-slice_fusion), channel_id=1, source_target_pairs={{4,0},{8,4},{12,8},{0,12},{5,1},{9,5},{13,9},{1,13},{6,2},{10,6},{... | collective-permute-start | bytes 1572872 | tf_op jit(solution)/shard_map/while/body/eval_jaxpr/ppermute | solution.py:18
  35.5 1.0 copy-start.2
  59.0 1.9 %copy-start.3 = (f32[4,64,512]{2,0,1:T(4,128)S(1)}, f32[4,64,512]{2,0,1:T(4,128)}, u32[]{:S(2)}) copy-start(f32[4,64,512]{2,0,1:T(4,128)} %copy.5) | copy-start | bytes 1572868
  59.0 1.9 %copy-start.4 = (f32[4,64,512]{2,0,1:T(4,128)S(1)}, f32[4,64,512]{2,0,1:T(4,128)}, u32[]{:S(2)}) copy-start(f32[4,64,512]{2,0,1:T(4,128)} %copy.9) | copy-start | bytes 1572868
  67.8 1.0 copy-start.5
Sparse Core Ops, SparseCore 0:
  70.1 25.9 reduce-scatter.1
where the time goes:
time: 105 us
  waiting for transfers between devices  35 us (33%)
  other arithmetic  32.7 us (31%)
  local copies, waits for them, and re-layouts  15.8 us (15%)
  between operations  13.6 us (13%)
  starting transfers between devices  5.05 us (5%)
  matrix products  2.46 us (2%)
    reduce_scatter x1, waiting for transfers between devices, local(): lax.psum_scatter(lag_terms(all_rows, inverse), ('day', 'seg'), scatter_di...  26.1 us
    another operation x3, other arithmetic  20.4 us
    gather x3, local copies, waits for them, and re-layouts, pair_spectrum(): source_rows = jnp.take(held_block, picked, axis=1)  9.31 us
    ppermute x2, waiting for transfers between devices, shifted(): return lax.ppermute(block, axis, route)  8.87 us
    reduce_sum x1, other arithmetic, pair_spectrum(): real_sum = jnp.sum(own_real * other_real + own_imag * other_imag, axis=0)  6.9 us
    ppermute x2, starting transfers between devices, shifted(): return lax.ppermute(block, axis, route)  5.05 us
    select_n x4, other arithmetic, pair_spectrum(): source_rows = jnp.take(held_block, picked, axis=1)  4.25 us
  transfers between devices with their start and end apart: 3, of which 3 were waited for; matrix products, arithmetic and copies ran while one was open for 13% of the time, Pallas kernels for 0%

commit v1 on v0

v1 whole, which is shorter than its diff:
```python
import functools
import math

import jax
import jax.numpy as jnp
import ml_dtypes
import numpy as np
from jax import lax
from jax.experimental import pallas as pl
from jax.experimental.pallas import tpu as pltpu
from jax.sharding import PartitionSpec as P

FREQS = 512
BAND = 64
LAGS = 256
SEGS = 4
WIDE = 128
CHUNKS = FREQS // WIDE
MESH = pl.DeviceIdType.MESH


def forward_chunks(samples):
    index = np.arange(samples)[:, None] * np.arange(FREQS)[None, :] % samples
    turns = index * (2.0 * math.pi / samples)
    table = np.stack([np.cos(turns), -np.sin(turns)], 1).reshape(samples, 2, CHUNKS, WIDE)
    return table.transpose(2, 0, 1, 3).reshape(CHUNKS, samples, 2 * WIDE).astype(ml_dtypes.bfloat16)


def inverse_chunks(samples):
    index = (np.arange(LAGS) - LAGS // 2)[:, None] * np.arange(FREQS)[None, :] % samples
    turns = index * (2.0 * math.pi / samples)
    table = np.stack([np.cos(turns), -np.sin(turns)], 1).reshape(LAGS, 2, CHUNKS, WIDE)
    return table.transpose(2, 0, 1, 3).reshape(CHUNKS, LAGS, 2 * WIDE).astype(ml_dtypes.bfloat16)


def selector(picks, sets, width):
    pick_count = picks.shape[0]
    across = lax.broadcasted_iota(jnp.int32, (width, width), 1)
    down = lax.broadcasted_iota(jnp.int32, (width, width), 0)
    columns = []
    for p in range(pick_count):
        row = picks[p : p + 1, :].astype(jnp.float32)
        diagonal = jnp.where(across == down, jnp.broadcast_to(row, (width, width)), 0.0)
        columns.append(jnp.sum(diagonal, axis=1, keepdims=True))
    column = jnp.concatenate(columns, 0)
    place = lax.broadcasted_iota(jnp.int32, (pick_count * width, sets * width), 1).astype(jnp.float32)
    rows = [jnp.where(place == column + float(s * width), 1.0, 0.0) for s in range(sets)]
    return jnp.concatenate(rows, 0).astype(jnp.bfloat16)


def whiten(spectra):
    real_part = spectra[:, :WIDE]
    imag_part = spectra[:, WIDE:]
    square = real_part * real_part + imag_part * imag_part
    high = square.astype(jnp.bfloat16)
    low = (square - high.astype(jnp.float32)).astype(jnp.bfloat16)
    down = lax.broadcasted_iota(jnp.int32, (WIDE, WIDE), 0) // BAND
    across = lax.broadcasted_iota(jnp.int32, (WIDE, WIDE), 1) // BAND
    mean = jnp.where(down == across, 0.5 / BAND, 0.0).astype(jnp.bfloat16)
    power = jnp.dot(high, mean, preferred_element_type=jnp.float32)
    power += jnp.dot(low, mean, preferred_element_type=jnp.float32)
    factor = lax.rsqrt(power + 1e-06)
    return jnp.concatenate([real_part * factor, imag_part * factor], 1).astype(jnp.bfloat16)


def cross_spectrum(own, other, select, sets, width):
    picked = jnp.dot(select, other, preferred_element_type=jnp.float32)
    rows = picked.shape[0] // sets
    picks = rows // width
    real_sum = jnp.zeros((rows, WIDE), jnp.float32)
    imag_sum = jnp.zeros((rows, WIDE), jnp.float32)
    for s in range(sets):
        mine = own[s * width : (s + 1) * width].astype(jnp.float32)
        mine = jnp.concatenate([mine] * picks, 0)
        theirs = picked[s * rows : (s + 1) * rows]
        mine_re, mine_im = mine[:, :WIDE], mine[:, WIDE:]
        their_re, their_im = theirs[:, :WIDE], theirs[:, WIDE:]
        real_sum += mine_re * their_re + mine_im * their_im
        imag_sum += mine_re * their_im - mine_im * their_re
    return jnp.concatenate([real_sum, imag_sum], 1).astype(jnp.bfloat16)


def lag_terms(table, cross):
    return lax.dot_general(table, cross, (((1,), (1,)), ((), ())), preferred_element_type=jnp.float32)


def kernel(
    dims, records_hbm, visits, forward_hbm, inverse_hbm, out,
    records, forward, inverse, whitened, held, held_visits, own_select, held_select, terms,
    early_out, late_out, back_out, early_in, late_in, back_in,
    load_sem, table_sem, block_send, block_recv, visit_send, visit_recv,
    early_send, early_recv, late_send, late_recv, back_send, back_recv,
):
    reach, days, segs, blocks, sets, width, picks, scale = dims
    groups = days * segs
    share = LAGS // groups
    cols = picks * width
    chan = lax.axis_index("chan")
    group = lax.axis_index("day") * segs + lax.axis_index("seg")

    def at(offset, step):
        other = lax.rem(group + step, groups)
        return {"chan": lax.rem(chan + offset + blocks, blocks), "day": other // segs, "seg": lax.rem(other, segs)}

    load_records = pltpu.make_async_copy(records_hbm, records, load_sem.at[0])
    load_inverse = pltpu.make_async_copy(inverse_hbm, inverse, load_sem.at[1])
    load_table = [
        pltpu.make_async_copy(forward_hbm.at[c], forward.at[c], table_sem.at[c]) for c in range(CHUNKS)
    ]
    load_records.start()
    load_table[0].start()

    barrier = pltpu.get_barrier_semaphore()
    partners = [(o, k) for o in range(-reach, reach + 1) for k in range(groups) if (o, k) != (0, 0)]
    for o, k in partners:
        pl.semaphore_signal(barrier, inc=1, device_id=at(o, k), device_id_type=MESH)
    for c in range(1, CHUNKS):
        load_table[c].start()
    load_inverse.start()

    for o in range(reach + 1):
        own_select[o] = selector(visits[reach + o], sets, width)

    send_visits, send_blocks = [], []
    load_records.wait()
    for c in range(CHUNKS):
        load_table[c].wait()
        spectra = jnp.dot(records[...], forward[c], preferred_element_type=jnp.float32)
        whitened[c] = whiten(spectra)
        if c == 0:
            pl.semaphore_wait(barrier, len(partners))
            for o in range(1, reach + 1):
                copy = pltpu.make_async_remote_copy(
                    visits.at[reach - o], held_visits.at[o - 1], visit_send.at[o - 1], visit_recv.at[o - 1],
                    device_id=at(o, 0), device_id_type=MESH,
                )
                copy.start()
                send_visits.append(copy)
        for o in range(1, reach + 1):
            copy = pltpu.make_async_remote_copy(
                whitened.at[c], held.at[o - 1, c], block_send.at[o - 1, c], block_recv.at[o - 1, c],
                device_id=at(o, 0), device_id_type=MESH,
            )
            copy.start()
            send_blocks.append(copy)
        if c == 0:
            load_inverse.wait()
        mine = whitened[c]
        cross = cross_spectrum(mine, mine, own_select[0], sets, width)
        part = lag_terms(inverse[c], cross).reshape(groups, share, cols)
        terms[reach] = part if c == 0 else terms[reach] + part

    early_out[...] = terms[reach].astype(jnp.bfloat16)
    send_results = []

    def send_result(source, target, send, recv, offset, step):
        other = lax.rem(group + step, groups)
        copy = pltpu.make_async_remote_copy(
            source.at[other], target.at[step], send.at[step], recv.at[step],
            device_id=at(offset, step), device_id_type=MESH,
        )
        copy.start()
        send_results.append(copy)

    for k in range(1, groups):
        send_result(early_out, early_in, early_send, early_recv, 0, k)

    for o in range(1, reach + 1):
        send_visits[o - 1].wait_recv()
        held_select[o - 1] = selector(held_visits[o - 1], sets, width)

    for c in range(CHUNKS):
        for o in range(1, reach + 1):
            send_blocks[c * reach + o - 1].wait_recv()
            mine, theirs = whitened[c], held[o - 1, c]
            down = cross_spectrum(mine, theirs, own_select[o], sets, width)
            up = cross_spectrum(theirs, mine, held_select[o - 1], sets, width)
            part = lag_terms(inverse[c], jnp.concatenate([down, up], 0))
            for place, piece in ((reach + o, part[:, :cols]), (reach - o, part[:, cols:])):
                piece = piece.reshape(groups, share, cols)
                terms[place] = piece if c == 0 else terms[place] + piece

    for o in range(1, reach + 1):
        back_out[o - 1] = terms[reach - o].astype(jnp.bfloat16)
        for k in range(groups):
            send_result(back_out.at[o - 1], back_in.at[o - 1], back_send.at[o - 1], back_recv.at[o - 1], -o, k)
        late_out[:, :, (o - 1) * cols : o * cols] = terms[reach + o].astype(jnp.bfloat16)
    for k in range(1, groups):
        send_result(late_out, late_in, late_send, late_recv, 0, k)

    for copy in send_results:
        copy.wait_recv()
    total = terms[reach, group]
    for k in range(1, groups):
        total += early_in[k].astype(jnp.float32)
    out[:, reach * cols : (reach + 1) * cols] = (total * scale).astype(jnp.bfloat16)
    for o in range(1, reach + 1):
        total = back_in[o - 1, 0].astype(jnp.float32)
        for k in range(1, groups):
            total += back_in[o - 1, k].astype(jnp.float32)
        out[:, (reach - o) * cols : (reach - o + 1) * cols] = (total * scale).astype(jnp.bfloat16)
        total = terms[reach + o, group]
        for k in range(1, groups):
            total += late_in[k, :, (o - 1) * cols : o * cols].astype(jnp.float32)
        out[:, (reach + o) * cols : (reach + o + 1) * cols] = (total * scale).astype(jnp.bfloat16)
    for copy in send_visits + send_blocks + send_results:
        copy.wait_send()


def local(records, visits):
    day_local, seg_local, width, samples = records.shape
    visit_count, picks, _ = visits.shape
    days, segs, blocks = lax.axis_size("day"), lax.axis_size("seg"), lax.axis_size("chan")
    reach = blocks // 4
    groups = days * segs
    share = LAGS // groups
    sets = day_local * seg_local
    rows = sets * width
    cols = picks * width
    scale = 1.0 / math.sqrt(FREQS * day_local * days * SEGS)
    bf16, f32 = jnp.bfloat16, jnp.float32
    hbm = pl.BlockSpec(memory_space=pl.ANY)
    vmem = pl.BlockSpec(memory_space=pltpu.VMEM)
    dma = pltpu.SemaphoreType.DMA
    flops = 2 * rows * samples * 2 * FREQS + 2 * LAGS * 2 * FREQS * visit_count * cols
    result = pl.pallas_call(
        functools.partial(kernel, (reach, days, segs, blocks, sets, width, picks, scale)),
        out_shape=jax.ShapeDtypeStruct((share, visit_count * cols), bf16),
        in_specs=[hbm, vmem, hbm, hbm],
        out_specs=vmem,
        scratch_shapes=[
            pltpu.VMEM((rows, samples), bf16),
            pltpu.VMEM((CHUNKS, samples, 2 * WIDE), bf16),
            pltpu.VMEM((CHUNKS, LAGS, 2 * WIDE), bf16),
            pltpu.VMEM((CHUNKS, rows, 2 * WIDE), bf16),
            pltpu.VMEM((reach, CHUNKS, rows, 2 * WIDE), bf16),
            pltpu.VMEM((reach, picks, width), jnp.int32),
            pltpu.VMEM((reach + 1, sets * cols, rows), bf16),
            pltpu.VMEM((reach, sets * cols, rows), bf16),
            pltpu.VMEM((visit_count, groups, share, cols), f32),
            pltpu.VMEM((groups, share, cols), bf16),
            pltpu.VMEM((groups, share, reach * cols), bf16),
            pltpu.VMEM((reach, groups, share, cols), bf16),
            pltpu.VMEM((groups, share, cols), bf16),
            pltpu.VMEM((groups, share, reach * cols), bf16),
            pltpu.VMEM((reach, groups, share, cols), bf16),
            dma((2,)), dma((CHUNKS,)), dma((reach, CHUNKS)), dma((reach, CHUNKS)), dma((reach,)), dma((reach,)),
            dma((groups,)), dma((groups,)), dma((groups,)), dma((groups,)),
            dma((reach, groups)), dma((reach, groups)),
        ],
        compiler_params=pltpu.CompilerParams(
            collective_id=0, has_side_effects=True, vmem_limit_bytes=48 * 1024 * 1024
        ),
        cost_estimate=pl.CostEstimate(flops=flops, bytes_accessed=8 * 1024 * 1024, transcendentals=0),
        name="correlate",
    )(records.reshape(rows, samples), visits, forward_chunks(samples), inverse_chunks(samples))
    return result.reshape(share, visit_count, picks, width)


def solution(mesh):
    in_specs = (P("day", "seg", ("grp", "chan"), None), P(None, None, ("grp", "chan")))
    out_specs = P(("day", "seg"), None, None, ("grp", "chan"))
    return jax.shard_map(local, mesh=mesh, in_specs=in_specs, out_specs=out_specs, check_vma=False)
```

time: 105 us -> 29.8 us (0.28)
  waiting for transfers between devices: 35 us -> 0 us
  other arithmetic: 32.7 us -> 0 us
  Pallas kernels: 0 us -> 23.6 us
  between operations: 13.6 us -> 0.01 us
  local copies, waits for them, and re-layouts: 15.8 us -> 5.9 us
  starting transfers between devices: 5.05 us -> 0 us
  matrix products: 2.46 us -> 0 us
    reduce_scatter x1 -> x0, waiting for transfers between devices: 26.1 us -> none  [local(): lax.psum_scatter(lag_terms(all_rows, inverse), ('day', 'seg'), scatter_di...]
    pallas_call x0 -> x1, Pallas kernels: none -> 23.6 us  [local(): pl.pallas_call(functools.partial(kernel, (reach, days, segs, blocks, sets...]
    another operation x3 -> x0, other arithmetic: 20.4 us -> none
    gather x3 -> x0, local copies, waits for them, and re-layouts: 9.31 us -> none  [pair_spectrum(): source_rows = jnp.take(held_block, picked, axis=1)]
    ppermute x2 -> x0, waiting for transfers between devices: 8.87 us -> none  [shifted(): return lax.ppermute(block, axis, route)]
    reduce_sum x2 -> x0, other arithmetic: 6.95 us -> none  [the longest x1 6.9 us: pair_spectrum(): real_sum = jnp.sum(own_real * other_real + own_imag * other_imag, axis=0)]
    ppermute x2 -> x0, starting transfers between devices: 5.05 us -> none  [shifted(): return lax.ppermute(block, axis, route)]
    select_n x4 -> x0, other arithmetic: 4.25 us -> none  [pair_spectrum(): source_rows = jnp.take(held_block, picked, axis=1)]
  transfers between devices with their start and end apart: 3 -> 0, of which waited for: 3 -> 0; matrix products, arithmetic and copies ran while one was open for 13% -> 0% of each run, Pallas kernels for 0% -> 0%
where the time goes in v1:
time: 29.8 us; the launch traced here: 29.5 us
  Pallas kernels  23.6 us (79%)
  local copies, waits for them, and re-layouts  5.9 us (20%)
    pallas_call x1, Pallas kernels, local(): pl.pallas_call(functools.partial(kernel, (reach, days, segs, blocks, sets...  23.6 us
    unnamed x8, local copies, waits for them, and re-layouts  5.14 us
    reshape x1, local copies, waits for them, and re-layouts, local(): return result.reshape(share, visit_count, picks, width)  0.76 us

profile of v1, /device:TPU:0, one launch (start us, length us, event | category | flops | bytes accessed | tf_op | source)
XLA Modules:
  0.0 29.5 jit_solution(8934710760741283108)
XLA Ops:
  0.0 0.0 copy-start
  0.0 2.2 %copy-done = bf16[4,2048,256]{2,1,0:T(8,128)(2,1)S(1)} copy-done((bf16[4,2048,256]{2,1,0:T(8,128)(2,1)S(1)}, bf16[4,2048,256]{2,1,0:T(8,128)(2,1)}, u32[]{:S(2)}) %copy-start) | copy-done | bytes 4194328
  2.2 0.0 copy-start.1
  2.2 1.2 %copy-done.1 = bf16[2,2,64,2048]{3,2,1,0:T(8,128)(2,1)S(1)} copy-done((bf16[2,2,64,2048]{3,2,1,0:T(8,128)(2,1)S(1)}, bf16[2,2,64,2048]{3,2,1,0:T(8,128)(2,1)}, u32[]{:S(2)}) %copy-start.1) | copy-done | bytes 1048600
  3.4 0.0 copy-start.2
  3.4 1.0 %copy-done.2 = bf16[4,256,256]{2,1,0:T(8,128)(2,1)S(1)} copy-done((bf16[4,256,256]{2,1,0:T(8,128)(2,1)S(1)}, bf16[4,256,256]{2,1,0:T(8,128)(2,1)}, u32[]{:S(2)}) %copy-start.2) | copy-done | bytes 524312
  4.5 0.0 copy-start.3
  4.5 0.7 %copy-done.3 = s32[3,2,64]{2,1,0:T(2,128)S(1)} copy-done((s32[3,2,64]{2,1,0:T(2,128)S(1)}, s32[3,2,64]{2,1,0:T(2,128)}, u32[]{:S(2)}) %copy-start.3) | copy-done | bytes 1560
  5.1 23.6 %correlate.1 = bf16[64,384]{1,0:T(8,128)(2,1)S(1)} custom-call(bf16[256,2048]{1,0:T(8,128)(2,1)S(1)} %bitcast.1, s32[3,2,64]{2,1,0:T(2,128)S(1)} %copy-done.3, bf16[4,2048,256]{2,1,0:T(8,128)(2,1)S(1)} %copy-done, bf16[4,256,256]{2,1,0:T(8,128)(2,1)S(1)} %copy-done.2), custom_call_target="tpu_custom_call" | custom-call | flops 1275068416 | bytes 8388608 | tf_op jit(solution)/shard_map/correlate/pallas_call | solution.py:226
  28.7 0.8 %reshape.7 = bf16[64,3,2,64]{3,2,1,0:T(2,128)(2,1)} reshape(bf16[64,384]{1,0:T(8,128)(2,1)S(1)} %correlate.1) | data formatting | bytes 98304 | tf_op jit(solution)/shard_map/reshape | solution.py:257
Async XLA Ops:
  0.0 2.2 %copy-start = (bf16[4,2048,256]{2,1,0:T(8,128)(2,1)S(1)}, bf16[4,2048,256]{2,1,0:T(8,128)(2,1)}, u32[]{:S(2)}) copy-start(bf16[4,2048,256]{2,1,0:T(8,128)(2,1)} %constant.4.clone.forward_hbm) | copy-start | bytes 12582916
  2.2 1.2 %copy-start.1 = (bf16[2,2,64,2048]{3,2,1,0:T(8,128)(2,1)S(1)}, bf16[2,2,64,2048]{3,2,1,0:T(8,128)(2,1)}, u32[]{:S(2)}) copy-start(bf16[2,2,64,2048]{3,2,1,0:T(8,128)(2,1)} %param.4) | copy-start | bytes 3145732
  3.4 1.0 %copy-start.2 = (bf16[4,256,256]{2,1,0:T(8,128)(2,1)S(1)}, bf16[4,256,256]{2,1,0:T(8,128)(2,1)}, u32[]{:S(2)}) copy-start(bf16[4,256,256]{2,1,0:T(8,128)(2,1)} %constant.5.clone.inverse_hbm) | copy-start | bytes 1572868
  4.5 0.7 %copy-start.3 = (s32[3,2,64]{2,1,0:T(2,128)S(1)}, s32[3,2,64]{2,1,0:T(2,128)}, u32[]{:S(2)}) copy-start(s32[3,2,64]{2,1,0:T(2,128)} %visits.1) | copy-start | bytes 4612

commit v2 on v1

--- a/solution.py
+++ b/solution.py
@@ -85,8 +85,8 @@
 
 
 def kernel(
-    dims, records_hbm, visits, forward_hbm, inverse_hbm, out,
-    records, forward, inverse, whitened, held, held_visits, own_select, held_select, terms,
+    dims, records_hbm, visits_hbm, forward_hbm, inverse_hbm, out,
+    visits, records, forward, inverse, whitened, held, held_visits, own_select, held_select, terms,
     early_out, late_out, back_out, early_in, late_in, back_in,
     load_sem, table_sem, block_send, block_recv, visit_send, visit_recv,
     early_send, early_recv, late_send, late_recv, back_send, back_recv,
@@ -104,9 +104,11 @@
 
     load_records = pltpu.make_async_copy(records_hbm, records, load_sem.at[0])
     load_inverse = pltpu.make_async_copy(inverse_hbm, inverse, load_sem.at[1])
+    load_visits = pltpu.make_async_copy(visits_hbm, visits, load_sem.at[2])
     load_table = [
         pltpu.make_async_copy(forward_hbm.at[c], forward.at[c], table_sem.at[c]) for c in range(CHUNKS)
     ]
+    load_visits.start()
     load_records.start()
     load_table[0].start()
 
@@ -118,6 +120,7 @@
         load_table[c].start()
     load_inverse.start()
 
+    load_visits.wait()
     for o in range(reach + 1):
         own_select[o] = selector(visits[reach + o], sets, width)
 
@@ -219,16 +222,17 @@
     cols = picks * width
     scale = 1.0 / math.sqrt(FREQS * day_local * days * SEGS)
     bf16, f32 = jnp.bfloat16, jnp.float32
-    hbm = pl.BlockSpec(memory_space=pl.ANY)
+    hbm = pl.BlockSpec(memory_space=pltpu.HBM)
     vmem = pl.BlockSpec(memory_space=pltpu.VMEM)
     dma = pltpu.SemaphoreType.DMA
     flops = 2 * rows * samples * 2 * FREQS + 2 * LAGS * 2 * FREQS * visit_count * cols
     result = pl.pallas_call(
         functools.partial(kernel, (reach, days, segs, blocks, sets, width, picks, scale)),
         out_shape=jax.ShapeDtypeStruct((share, visit_count * cols), bf16),
-        in_specs=[hbm, vmem, hbm, hbm],
+        in_specs=[hbm, hbm, hbm, hbm],
         out_specs=vmem,
         scratch_shapes=[
+            pltpu.VMEM((visit_count, picks, width), jnp.int32),
             pltpu.VMEM((rows, samples), bf16),
             pltpu.VMEM((CHUNKS, samples, 2 * WIDE), bf16),
             pltpu.VMEM((CHUNKS, LAGS, 2 * WIDE), bf16),
@@ -244,12 +248,12 @@
             pltpu.VMEM((groups, share, cols), bf16),
             pltpu.VMEM((groups, share, reach * cols), bf16),
             pltpu.VMEM((reach, groups, share, cols), bf16),
-            dma((2,)), dma((CHUNKS,)), dma((reach, CHUNKS)), dma((reach, CHUNKS)), dma((reach,)), dma((reach,)),
+            dma((3,)), dma((CHUNKS,)), dma((reach, CHUNKS)), dma((reach, CHUNKS)), dma((reach,)), dma((reach,)),
             dma((groups,)), dma((groups,)), dma((groups,)), dma((groups,)),
             dma((reach, groups)), dma((reach, groups)),
         ],
         compiler_params=pltpu.CompilerParams(
-            collective_id=0, has_side_effects=True, vmem_limit_bytes=48 * 1024 * 1024
+            collective_id=0, has_side_effects=True, vmem_limit_bytes=56 * 1024 * 1024
         ),
         cost_estimate=pl.CostEstimate(flops=flops, bytes_accessed=8 * 1024 * 1024, transcendentals=0),
         name="correlate",

time: 29.8 us -> 26.1 us (0.88)
  local copies, waits for them, and re-layouts: 5.9 us -> 1.56 us
  Pallas kernels: 23.6 us -> 24.3 us
    unnamed x8 -> x0, local copies, waits for them, and re-layouts: 5.14 us -> none
    reshape x1, local copies, waits for them, and re-layouts: 0.76 us -> 1.56 us  [local(): return result.reshape(share, visit_count, picks, width)]
    pallas_call x1, Pallas kernels: 23.6 us -> 24.3 us  [local(): pl.pallas_call(functools.partial(kernel, (reach, days, segs, blocks, sets...]
where the time goes in v2:
time: 26.1 us; the launch traced here: 25.9 us
  Pallas kernels  24.3 us (93%)
  local copies, waits for them, and re-layouts  1.56 us (6%)
    pallas_call x1, Pallas kernels, local(): pl.pallas_call(functools.partial(kernel, (reach, days, segs, blocks, sets...  24.3 us
    reshape x1, local copies, waits for them, and re-layouts, local(): return result.reshape(share, visit_count, picks, width)  1.56 us

profile of v2, /device:TPU:0, one launch (start us, length us, event | category | flops | bytes accessed | tf_op | source)
XLA Modules:
  0.0 25.9 jit_solution(2725090762559225383)
XLA Ops:
  0.0 24.3 %correlate.1 = bf16[64,384]{1,0:T(8,128)(2,1)} custom-call(bf16[256,2048]{1,0:T(8,128)(2,1)} %bitcast.1, s32[3,2,64]{2,1,0:T(2,128)} %visits_hbm.1, bf16[4,2048,256]{2,1,0:T(8,128)(2,1)} %constant.4.clone.forward_hbm, bf16[4,256,256]{2,1,0:T(8,128)(2,1)} %constant.5.clone.inverse_hbm), custom_call_target="tpu_custom_call" | custom-call | flops 1275068416 | bytes 8388608 | tf_op jit(solution)/shard_map/correlate/pallas_call | solution.py:229
  24.3 1.6 %reshape.7 = bf16[64,3,2,64]{3,2,1,0:T(2,128)(2,1)} reshape(bf16[64,384]{1,0:T(8,128)(2,1)} %correlate.1) | data formatting | bytes 98304 | tf_op jit(solution)/shard_map/reshape | solution.py:261

commit v3 on v2

--- a/solution.py
+++ b/solution.py
@@ -63,21 +63,21 @@
     return jnp.concatenate([real_part * factor, imag_part * factor], 1).astype(jnp.bfloat16)
 
 
-def cross_spectrum(own, other, select, sets, width):
+def cross_sums(own, other, select, width):
+    sets = own.shape[0] // width
     picked = jnp.dot(select, other, preferred_element_type=jnp.float32)
     rows = picked.shape[0] // sets
-    picks = rows // width
     real_sum = jnp.zeros((rows, WIDE), jnp.float32)
     imag_sum = jnp.zeros((rows, WIDE), jnp.float32)
     for s in range(sets):
         mine = own[s * width : (s + 1) * width].astype(jnp.float32)
-        mine = jnp.concatenate([mine] * picks, 0)
+        mine = jnp.concatenate([mine] * (rows // width), 0)
         theirs = picked[s * rows : (s + 1) * rows]
         mine_re, mine_im = mine[:, :WIDE], mine[:, WIDE:]
         their_re, their_im = theirs[:, :WIDE], theirs[:, WIDE:]
         real_sum += mine_re * their_re + mine_im * their_im
         imag_sum += mine_re * their_im - mine_im * their_re
-    return jnp.concatenate([real_sum, imag_sum], 1).astype(jnp.bfloat16)
+    return jnp.concatenate([real_sum, imag_sum], 1)
 
 
 def lag_terms(table, cross):
@@ -120,18 +120,31 @@
         load_table[c].start()
     load_inverse.start()
 
-    load_visits.wait()
-    for o in range(reach + 1):
-        own_select[o] = selector(visits[reach + o], sets, width)
-
-    send_visits, send_blocks = [], []
+    halves = [(0, sets // 2), (sets // 2, sets // 2)] if sets % 2 == 0 else [(0, sets)]
+    pieces = [halves if c in (0, CHUNKS - 1) else [(0, sets)] for c in range(CHUNKS)]
+
+    def block_rows(piece):
+        return pl.ds(piece[0] * width, piece[1] * width)
+
+    send_visits, send_blocks = [], {}
     load_records.wait()
     for c in range(CHUNKS):
         load_table[c].wait()
-        spectra = jnp.dot(records[...], forward[c], preferred_element_type=jnp.float32)
-        whitened[c] = whiten(spectra)
+        for i, piece in enumerate(pieces[c]):
+            spectra = jnp.dot(records[block_rows(piece)], forward[c], preferred_element_type=jnp.float32)
+            whitened[c, block_rows(piece)] = whiten(spectra)
+            if c == 0 and i == 0:
+                pl.semaphore_wait(barrier, len(partners))
+            for o in range(1, reach + 1):
+                copy = pltpu.make_async_remote_copy(
+                    whitened.at[c, block_rows(piece)], held.at[o - 1, c, block_rows(piece)],
+                    block_send.at[o - 1, c, i], block_recv.at[o - 1, c, i],
+                    device_id=at(o, 0), device_id_type=MESH,
+                )
+                copy.start()
+                send_blocks[c, o, i] = copy
         if c == 0:
-            pl.semaphore_wait(barrier, len(partners))
+            load_visits.wait()
             for o in range(1, reach + 1):
                 copy = pltpu.make_async_remote_copy(
                     visits.at[reach - o], held_visits.at[o - 1], visit_send.at[o - 1], visit_recv.at[o - 1],
@@ -139,21 +152,14 @@
                 )
                 copy.start()
                 send_visits.append(copy)
-        for o in range(1, reach + 1):
-            copy = pltpu.make_async_remote_copy(
-                whitened.at[c], held.at[o - 1, c], block_send.at[o - 1, c], block_recv.at[o - 1, c],
-                device_id=at(o, 0), device_id_type=MESH,
-            )
-            copy.start()
-            send_blocks.append(copy)
-        if c == 0:
+            for o in range(reach + 1):
+                own_select[o] = selector(visits[reach + o], sets, width)
             load_inverse.wait()
         mine = whitened[c]
-        cross = cross_spectrum(mine, mine, own_select[0], sets, width)
+        cross = cross_sums(mine, mine, own_select[0], width).astype(jnp.bfloat16)
         part = lag_terms(inverse[c], cross).reshape(groups, share, cols)
         terms[reach] = part if c == 0 else terms[reach] + part
 
-    early_out[...] = terms[reach].astype(jnp.bfloat16)
     send_results = []
 
     def send_result(source, target, send, recv, offset, step):
@@ -164,49 +170,56 @@
         )
         copy.start()
         send_results.append(copy)
-
-    for k in range(1, groups):
-        send_result(early_out, early_in, early_send, early_recv, 0, k)
+        return copy
+
+    def finish(place, total, copies, target):
+        for copy, k in copies:
+            copy.wait_recv()
+            total += target[k].astype(jnp.float32)
+        out[:, place * cols : (place + 1) * cols] = (total * scale).astype(jnp.bfloat16)
+
+    early_out[...] = terms[reach].astype(jnp.bfloat16)
+    early = [(send_result(early_out, early_in, early_send, early_recv, 0, k), k) for k in range(1, groups)]
 
     for o in range(1, reach + 1):
         send_visits[o - 1].wait_recv()
         held_select[o - 1] = selector(held_visits[o - 1], sets, width)
 
+    back, late = {}, {}
     for c in range(CHUNKS):
+        if c == CHUNKS - 1:
+            finish(reach, terms[reach, group], early, early_in)
         for o in range(1, reach + 1):
-            send_blocks[c * reach + o - 1].wait_recv()
-            mine, theirs = whitened[c], held[o - 1, c]
-            down = cross_spectrum(mine, theirs, own_select[o], sets, width)
-            up = cross_spectrum(theirs, mine, held_select[o - 1], sets, width)
-            part = lag_terms(inverse[c], jnp.concatenate([down, up], 0))
-            for place, piece in ((reach + o, part[:, :cols]), (reach - o, part[:, cols:])):
-                piece = piece.reshape(groups, share, cols)
-                terms[place] = piece if c == 0 else terms[place] + piece
+            up, down = 0.0, 0.0
+            for i, piece in enumerate(pieces[c]):
+                send_blocks[c, o, i].wait_recv()
+                mine, theirs = whitened[c, block_rows(piece)], held[o - 1, c, block_rows(piece)]
+                part = (slice(0, piece[1] * cols), slice(0, piece[1] * width))
+                up += cross_sums(theirs, mine, held_select[o - 1][part], width)
+                if c == CHUNKS - 1 and i == len(pieces[c]) - 1:
+                    last = lag_terms(inverse[c], up.astype(jnp.bfloat16)).reshape(groups, share, cols)
+                    back_out[o - 1] = (terms[reach - o] + last).astype(jnp.bfloat16)
+                    refs = [ref.at[o - 1] for ref in (back_out, back_in, back_send, back_recv)]
+                    back[o] = [(send_result(*refs, -o, k), k) for k in range(groups)]
+                down += cross_sums(mine, theirs, own_select[o][part], width)
+            if c < CHUNKS - 1:
+                both = jnp.concatenate([down, up], 0).astype(jnp.bfloat16)
+                both = lag_terms(inverse[c], both)
+                for place, piece in ((reach + o, both[:, :cols]), (reach - o, both[:, cols:])):
+                    piece = piece.reshape(groups, share, cols)
+                    terms[place] = piece if c == 0 else terms[place] + piece
+            else:
+                last = lag_terms(inverse[c], down.astype(jnp.bfloat16)).reshape(groups, share, cols)
+                last += terms[reach + o]
+                terms[reach + o] = last
+                late_out[o - 1] = last.astype(jnp.bfloat16)
+                refs = [ref.at[o - 1] for ref in (late_out, late_in, late_send, late_recv)]
+                late[o] = [(send_result(*refs, 0, k), k) for k in range(1, groups)]
 
     for o in range(1, reach + 1):
-        back_out[o - 1] = terms[reach - o].astype(jnp.bfloat16)
-        for k in range(groups):
-            send_result(back_out.at[o - 1], back_in.at[o - 1], back_send.at[o - 1], back_recv.at[o - 1], -o, k)
-        late_out[:, :, (o - 1) * cols : o * cols] = terms[reach + o].astype(jnp.bfloat16)
-    for k in range(1, groups):
-        send_result(late_out, late_in, late_send, late_recv, 0, k)
-
-    for copy in send_results:
-        copy.wait_recv()
-    total = terms[reach, group]
-    for k in range(1, groups):
-        total += early_in[k].astype(jnp.float32)
-    out[:, reach * cols : (reach + 1) * cols] = (total * scale).astype(jnp.bfloat16)
-    for o in range(1, reach + 1):
-        total = back_in[o - 1, 0].astype(jnp.float32)
-        for k in range(1, groups):
-            total += back_in[o - 1, k].astype(jnp.float32)
-        out[:, (reach - o) * cols : (reach - o + 1) * cols] = (total * scale).astype(jnp.bfloat16)
-        total = terms[reach + o, group]
-        for k in range(1, groups):
-            total += late_in[k, :, (o - 1) * cols : o * cols].astype(jnp.float32)
-        out[:, (reach + o) * cols : (reach + o + 1) * cols] = (total * scale).astype(jnp.bfloat16)
-    for copy in send_visits + send_blocks + send_results:
+        finish(reach - o, 0.0, back[o], back_in.at[o - 1])
+        finish(reach + o, terms[reach + o, group], late[o], late_in.at[o - 1])
+    for copy in send_visits + list(send_blocks.values()) + send_results:
         copy.wait_send()
 
 
@@ -243,17 +256,17 @@
             pltpu.VMEM((reach, sets * cols, rows), bf16),
             pltpu.VMEM((visit_count, groups, share, cols), f32),
             pltpu.VMEM((groups, share, cols), bf16),
-            pltpu.VMEM((groups, share, reach * cols), bf16),
+            pltpu.VMEM((reach, groups, share, cols), bf16),
             pltpu.VMEM((reach, groups, share, cols), bf16),
             pltpu.VMEM((groups, share, cols), bf16),
-            pltpu.VMEM((groups, share, reach * cols), bf16),
-            pltpu.VMEM((reach, groups, share, cols), bf16),
-            dma((3,)), dma((CHUNKS,)), dma((reach, CHUNKS)), dma((reach, CHUNKS)), dma((reach,)), dma((reach,)),
-            dma((groups,)), dma((groups,)), dma((groups,)), dma((groups,)),
+            pltpu.VMEM((reach, groups, share, cols), bf16),
+            pltpu.VMEM((reach, groups, share, cols), bf16),
+            dma((3,)), dma((CHUNKS,)), dma((reach, CHUNKS, 2)), dma((reach, CHUNKS, 2)), dma((reach,)), dma((reach,)),
+            dma((groups,)), dma((groups,)), dma((reach, groups)), dma((reach, groups)),
             dma((reach, groups)), dma((reach, groups)),
         ],
         compiler_params=pltpu.CompilerParams(
-            collective_id=0, has_side_effects=True, vmem_limit_bytes=56 * 1024 * 1024
+            collective_id=0, has_side_effects=True, vmem_limit_bytes=32 * 1024 * 1024
         ),
         cost_estimate=pl.CostEstimate(flops=flops, bytes_accessed=8 * 1024 * 1024, transcendentals=0),
         name="correlate",

time: 26.1 us -> 29.6 us (1.13)
  local copies, waits for them, and re-layouts: 1.56 us -> 5.9 us
  Pallas kernels: 24.3 us -> 23.4 us
    unnamed x0 -> x8, local copies, waits for them, and re-layouts: none -> 5.14 us
    pallas_call x1, Pallas kernels: 24.3 us -> 23.4 us  [local(): pl.pallas_call(functools.partial(kernel, (reach, days, segs, blocks, sets...]
    reshape x1, local copies, waits for them, and re-layouts: 1.56 us -> 0.76 us  [local(): return result.reshape(share, visit_count, picks, width)]
where the time goes in v3:
time: 29.6 us; the launch traced here: 29.4 us
  Pallas kernels  23.4 us (79%)
  local copies, waits for them, and re-layouts  5.9 us (20%)
    pallas_call x1, Pallas kernels, local(): pl.pallas_call(functools.partial(kernel, (reach, days, segs, blocks, sets...  23.4 us
    unnamed x8, local copies, waits for them, and re-layouts  5.14 us
    reshape x1, local copies, waits for them, and re-layouts, local(): return result.reshape(share, visit_count, picks, width)  0.76 us

profile of v3, /device:TPU:0, one launch (start us, length us, event | category | flops | bytes accessed | tf_op | source)
XLA Modules:
  0.0 29.4 jit_solution(14674507541789099561)
XLA Ops:
  0.0 0.0 copy-start
  0.0 2.2 %copy-done = bf16[4,2048,256]{2,1,0:T(8,128)(2,1)S(1)} copy-done((bf16[4,2048,256]{2,1,0:T(8,128)(2,1)S(1)}, bf16[4,2048,256]{2,1,0:T(8,128)(2,1)}, u32[]{:S(2)}) %copy-start) | copy-done | bytes 4194328
  2.2 0.0 copy-start.1
  2.2 1.2 %copy-done.1 = bf16[2,2,64,2048]{3,2,1,0:T(8,128)(2,1)S(1)} copy-done((bf16[2,2,64,2048]{3,2,1,0:T(8,128)(2,1)S(1)}, bf16[2,2,64,2048]{3,2,1,0:T(8,128)(2,1)}, u32[]{:S(2)}) %copy-start.1) | copy-done | bytes 1048600
  3.4 0.0 copy-start.2
  3.4 1.0 %copy-done.2 = bf16[4,256,256]{2,1,0:T(8,128)(2,1)S(1)} copy-done((bf16[4,256,256]{2,1,0:T(8,128)(2,1)S(1)}, bf16[4,256,256]{2,1,0:T(8,128)(2,1)}, u32[]{:S(2)}) %copy-start.2) | copy-done | bytes 524312
  4.5 0.0 copy-start.3
  4.5 0.7 %copy-done.3 = s32[3,2,64]{2,1,0:T(2,128)S(1)} copy-done((s32[3,2,64]{2,1,0:T(2,128)S(1)}, s32[3,2,64]{2,1,0:T(2,128)}, u32[]{:S(2)}) %copy-start.3) | copy-done | bytes 1560
  5.1 23.4 %correlate.1 = bf16[64,384]{1,0:T(8,128)(2,1)S(1)} custom-call(bf16[256,2048]{1,0:T(8,128)(2,1)S(1)} %bitcast.1, s32[3,2,64]{2,1,0:T(2,128)S(1)} %copy-done.3, bf16[4,2048,256]{2,1,0:T(8,128)(2,1)S(1)} %copy-done, bf16[4,256,256]{2,1,0:T(8,128)(2,1)S(1)} %copy-done.2), custom_call_target="tpu_custom_call" | custom-call | flops 1275068416 | bytes 8388608 | tf_op jit(solution)/shard_map/correlate/pallas_call | solution.py:242
  28.6 0.8 %reshape.7 = bf16[64,3,2,64]{3,2,1,0:T(2,128)(2,1)} reshape(bf16[64,384]{1,0:T(8,128)(2,1)S(1)} %correlate.1) | data formatting | bytes 98304 | tf_op jit(solution)/shard_map/reshape | solution.py:274
Async XLA Ops:
  0.0 2.2 %copy-start = (bf16[4,2048,256]{2,1,0:T(8,128)(2,1)S(1)}, bf16[4,2048,256]{2,1,0:T(8,128)(2,1)}, u32[]{:S(2)}) copy-start(bf16[4,2048,256]{2,1,0:T(8,128)(2,1)} %constant.4.clone.forward_hbm) | copy-start | bytes 12582916
  2.2 1.2 %copy-start.1 = (bf16[2,2,64,2048]{3,2,1,0:T(8,128)(2,1)S(1)}, bf16[2,2,64,2048]{3,2,1,0:T(8,128)(2,1)}, u32[]{:S(2)}) copy-start(bf16[2,2,64,2048]{3,2,1,0:T(8,128)(2,1)} %param.4) | copy-start | bytes 3145732
  3.4 1.0 %copy-start.2 = (bf16[4,256,256]{2,1,0:T(8,128)(2,1)S(1)}, bf16[4,256,256]{2,1,0:T(8,128)(2,1)}, u32[]{:S(2)}) copy-start(bf16[4,256,256]{2,1,0:T(8,128)(2,1)} %constant.5.clone.inverse_hbm) | copy-start | bytes 1572868
  4.5 0.7 %copy-start.3 = (s32[3,2,64]{2,1,0:T(2,128)S(1)}, s32[3,2,64]{2,1,0:T(2,128)}, u32[]{:S(2)}) copy-start(s32[3,2,64]{2,1,0:T(2,128)} %visits_hbm.1) | copy-start | bytes 4612

commit v4 on v3

--- a/solution.py
+++ b/solution.py
@@ -239,6 +239,7 @@
     vmem = pl.BlockSpec(memory_space=pltpu.VMEM)
     dma = pltpu.SemaphoreType.DMA
     flops = 2 * rows * samples * 2 * FREQS + 2 * LAGS * 2 * FREQS * visit_count * cols
+    operands = (records.reshape(rows, samples), visits, forward_chunks(samples), inverse_chunks(samples))
     result = pl.pallas_call(
         functools.partial(kernel, (reach, days, segs, blocks, sets, width, picks, scale)),
         out_shape=jax.ShapeDtypeStruct((share, visit_count * cols), bf16),
@@ -270,7 +271,7 @@
         ),
         cost_estimate=pl.CostEstimate(flops=flops, bytes_accessed=8 * 1024 * 1024, transcendentals=0),
         name="correlate",
-    )(records.reshape(rows, samples), visits, forward_chunks(samples), inverse_chunks(samples))
+    )(*(pltpu.with_memory_space_constraint(jnp.asarray(x), pltpu.HBM) for x in operands))
     return result.reshape(share, visit_count, picks, width)
 
 

time: 29.6 us -> 24.5 us (0.83)
  local copies, waits for them, and re-layouts: 5.9 us -> 0.76 us
    unnamed x8 -> x0, local copies, waits for them, and re-layouts: 5.14 us -> none
where the time goes in v4:
time: 24.5 us; the launch traced here: 24.3 us
  Pallas kernels  23.6 us (96%)
  local copies, waits for them, and re-layouts  0.76 us (3%)
    pallas_call x1, Pallas kernels, local(): pl.pallas_call(functools.partial(kernel, (reach, days, segs, blocks, sets...  23.6 us
    reshape x1, local copies, waits for them, and re-layouts, local(): return result.reshape(share, visit_count, picks, width)  0.76 us

profile of v4, /device:TPU:0, one launch (start us, length us, event | category | flops | bytes accessed | tf_op | source)
XLA Modules:
  0.0 24.3 jit_solution(14540003174078031788)
XLA Ops:
  0.0 23.6 %correlate.1 = bf16[64,384]{1,0:T(8,128)(2,1)S(1)} custom-call(bf16[256,2048]{1,0:T(8,128)(2,1)} %bitcast.1, s32[3,2,64]{2,1,0:T(2,128)} %visits_hbm.1, bf16[4,2048,256]{2,1,0:T(8,128)(2,1)} %constant.4.clone.forward_hbm, bf16[4,256,256]{2,1,0:T(8,128)(2,1)} %constant.5.clone.inverse_hbm), custom_call_target="tpu_custom_call" | custom-call | flops 1275068416 | bytes 8388608 | tf_op jit(solution)/shard_map/correlate/pallas_call | solution.py:243
  23.6 0.8 %reshape.7 = bf16[64,3,2,64]{3,2,1,0:T(2,128)(2,1)} reshape(bf16[64,384]{1,0:T(8,128)(2,1)S(1)} %correlate.1) | data formatting | bytes 98304 | tf_op jit(solution)/shard_map/reshape | solution.py:275

commit v5 on v4

--- a/solution.py
+++ b/solution.py
@@ -20,10 +20,10 @@
 
 
 def forward_chunks(samples):
-    index = np.arange(samples)[:, None] * np.arange(FREQS)[None, :] % samples
+    index = np.arange(samples // 2)[:, None] * np.arange(FREQS)[None, :] % samples
     turns = index * (2.0 * math.pi / samples)
-    table = np.stack([np.cos(turns), -np.sin(turns)], 1).reshape(samples, 2, CHUNKS, WIDE)
-    return table.transpose(2, 0, 1, 3).reshape(CHUNKS, samples, 2 * WIDE).astype(ml_dtypes.bfloat16)
+    table = np.stack([np.cos(turns), -np.sin(turns)], 1).reshape(samples // 2, 2, CHUNKS, WIDE)
+    return table.transpose(2, 0, 1, 3).reshape(CHUNKS, samples // 2, 2 * WIDE).astype(ml_dtypes.bfloat16)
 
 
 def inverse_chunks(samples):
@@ -46,6 +46,14 @@
     place = lax.broadcasted_iota(jnp.int32, (pick_count * width, sets * width), 1).astype(jnp.float32)
     rows = [jnp.where(place == column + float(s * width), 1.0, 0.0) for s in range(sets)]
     return jnp.concatenate(rows, 0).astype(jnp.bfloat16)
+
+
+def transform(records, table):
+    half = table.shape[0]
+    first = jnp.dot(records[:, :half], table, preferred_element_type=jnp.float32)
+    second = jnp.dot(records[:, half:], table, preferred_element_type=jnp.float32)
+    odd = lax.broadcasted_iota(jnp.int32, first.shape, 1) % 2
+    return jnp.where(odd == 1, first - second, first + second)
 
 
 def whiten(spectra):
@@ -102,38 +110,44 @@
         other = lax.rem(group + step, groups)
         return {"chan": lax.rem(chan + offset + blocks, blocks), "day": other // segs, "seg": lax.rem(other, segs)}
 
-    load_records = pltpu.make_async_copy(records_hbm, records, load_sem.at[0])
-    load_inverse = pltpu.make_async_copy(inverse_hbm, inverse, load_sem.at[1])
-    load_visits = pltpu.make_async_copy(visits_hbm, visits, load_sem.at[2])
+    half = sets // 2
+    halves = [(0, half), (half, sets - half)] if sets > 1 else [(0, sets)]
+    parts = [(0, half), (half, sets - 1 - half), (sets - 1, 1)] if sets > 2 else halves
+    pieces = [halves if c == 0 else parts if c == CHUNKS - 1 else [(0, sets)] for c in range(CHUNKS)]
+
+    def block_rows(piece):
+        return pl.ds(piece[0] * width, piece[1] * width)
+
+    load_records = [
+        pltpu.make_async_copy(records_hbm.at[block_rows(piece)], records.at[block_rows(piece)], load_sem.at[2 + i])
+        for i, piece in enumerate(halves)
+    ]
+    load_inverse = pltpu.make_async_copy(inverse_hbm, inverse, load_sem.at[0])
+    load_visits = pltpu.make_async_copy(visits_hbm, visits, load_sem.at[1])
     load_table = [
         pltpu.make_async_copy(forward_hbm.at[c], forward.at[c], table_sem.at[c]) for c in range(CHUNKS)
     ]
+    load_table[0].start()
+    for copy in load_records:
+        copy.start()
     load_visits.start()
-    load_records.start()
-    load_table[0].start()
 
     barrier = pltpu.get_barrier_semaphore()
     partners = [(o, k) for o in range(-reach, reach + 1) for k in range(groups) if (o, k) != (0, 0)]
     for o, k in partners:
         pl.semaphore_signal(barrier, inc=1, device_id=at(o, k), device_id_type=MESH)
-    for c in range(1, CHUNKS):
-        load_table[c].start()
-    load_inverse.start()
-
-    halves = [(0, sets // 2), (sets // 2, sets // 2)] if sets % 2 == 0 else [(0, sets)]
-    pieces = [halves if c in (0, CHUNKS - 1) else [(0, sets)] for c in range(CHUNKS)]
-
-    def block_rows(piece):
-        return pl.ds(piece[0] * width, piece[1] * width)
-
     send_visits, send_blocks = [], {}
-    load_records.wait()
     for c in range(CHUNKS):
         load_table[c].wait()
         for i, piece in enumerate(pieces[c]):
-            spectra = jnp.dot(records[block_rows(piece)], forward[c], preferred_element_type=jnp.float32)
+            if c == 0:
+                load_records[i].wait()
+            spectra = transform(records[block_rows(piece)], forward[c])
             whitened[c, block_rows(piece)] = whiten(spectra)
             if c == 0 and i == 0:
+                load_inverse.start()
+                for later in range(1, CHUNKS):
+                    load_table[later].start()
                 pl.semaphore_wait(barrier, len(partners))
             for o in range(1, reach + 1):
                 copy = pltpu.make_async_remote_copy(
@@ -248,7 +262,7 @@
         scratch_shapes=[
             pltpu.VMEM((visit_count, picks, width), jnp.int32),
             pltpu.VMEM((rows, samples), bf16),
-            pltpu.VMEM((CHUNKS, samples, 2 * WIDE), bf16),
+            pltpu.VMEM((CHUNKS, samples // 2, 2 * WIDE), bf16),
             pltpu.VMEM((CHUNKS, LAGS, 2 * WIDE), bf16),
             pltpu.VMEM((CHUNKS, rows, 2 * WIDE), bf16),
             pltpu.VMEM((reach, CHUNKS, rows, 2 * WIDE), bf16),
@@ -262,7 +276,7 @@
             pltpu.VMEM((groups, share, cols), bf16),
             pltpu.VMEM((reach, groups, share, cols), bf16),
             pltpu.VMEM((reach, groups, share, cols), bf16),
-            dma((3,)), dma((CHUNKS,)), dma((reach, CHUNKS, 2)), dma((reach, CHUNKS, 2)), dma((reach,)), dma((reach,)),
+            dma((4,)), dma((CHUNKS,)), dma((reach, CHUNKS, 3)), dma((reach, CHUNKS, 3)), dma((reach,)), dma((reach,)),
             dma((groups,)), dma((groups,)), dma((reach, groups)), dma((reach, groups)),
             dma((reach, groups)), dma((reach, groups)),
         ],

time: 24.5 us -> 24.3 us (level)
  no operation moved by 1% of the time
where the time goes in v5:
time: 24.3 us; the launch traced here: 24.1 us
  Pallas kernels  23.4 us (96%)
  local copies, waits for them, and re-layouts  0.76 us (3%)
    pallas_call x1, Pallas kernels, local(): pl.pallas_call(functools.partial(kernel, (reach, days, segs, blocks, sets...  23.4 us
    reshape x1, local copies, waits for them, and re-layouts, local(): return result.reshape(share, visit_count, picks, width)  0.76 us

profile of v5, /device:TPU:0, one launch (start us, length us, event | category | flops | bytes accessed | tf_op | source)
XLA Modules:
  0.0 24.1 jit_solution(9174818730291797654)
XLA Ops:
  0.0 23.4 %correlate.1 = bf16[64,384]{1,0:T(8,128)(2,1)S(1)} custom-call(bf16[256,2048]{1,0:T(8,128)(2,1)} %bitcast.1, s32[3,2,64]{2,1,0:T(2,128)} %visits_hbm.1, bf16[4,1024,256]{2,1,0:T(8,128)(2,1)} %constant.4.clone.forward_hbm, bf16[4,256,256]{2,1,0:T(8,128)(2,1)} %constant.5.clone.inverse_hbm), custom_call_target="tpu_custom_call" | custom-call | flops 1275068416 | bytes 8388608 | tf_op jit(solution)/shard_map/correlate/pallas_call | solution.py:257
  23.4 0.8 %reshape.7 = bf16[64,3,2,64]{3,2,1,0:T(2,128)(2,1)} reshape(bf16[64,384]{1,0:T(8,128)(2,1)S(1)} %correlate.1) | data formatting | bytes 98304 | tf_op jit(solution)/shard_map/reshape | solution.py:289

commit v6 on v5

--- a/solution.py
+++ b/solution.py
@@ -136,39 +136,30 @@
     partners = [(o, k) for o in range(-reach, reach + 1) for k in range(groups) if (o, k) != (0, 0)]
     for o, k in partners:
         pl.semaphore_signal(barrier, inc=1, device_id=at(o, k), device_id_type=MESH)
-    send_visits, send_blocks = [], {}
-    for c in range(CHUNKS):
-        load_table[c].wait()
-        for i, piece in enumerate(pieces[c]):
-            if c == 0:
-                load_records[i].wait()
-            spectra = transform(records[block_rows(piece)], forward[c])
-            whitened[c, block_rows(piece)] = whiten(spectra)
-            if c == 0 and i == 0:
-                load_inverse.start()
-                for later in range(1, CHUNKS):
-                    load_table[later].start()
-                pl.semaphore_wait(barrier, len(partners))
-            for o in range(1, reach + 1):
-                copy = pltpu.make_async_remote_copy(
-                    whitened.at[c, block_rows(piece)], held.at[o - 1, c, block_rows(piece)],
-                    block_send.at[o - 1, c, i], block_recv.at[o - 1, c, i],
-                    device_id=at(o, 0), device_id_type=MESH,
-                )
-                copy.start()
-                send_blocks[c, o, i] = copy
-        if c == 0:
-            load_visits.wait()
-            for o in range(1, reach + 1):
-                copy = pltpu.make_async_remote_copy(
-                    visits.at[reach - o], held_visits.at[o - 1], visit_send.at[o - 1], visit_recv.at[o - 1],
-                    device_id=at(o, 0), device_id_type=MESH,
-                )
-                copy.start()
-                send_visits.append(copy)
-            for o in range(reach + 1):
-                own_select[o] = selector(visits[reach + o], sets, width)
-            load_inverse.wait()
+    order = [(c, i) for c in range(CHUNKS) for i in range(len(pieces[c]))]
+    send_visits, send_blocks, sent = [], {}, set()
+
+    def left(c, i):
+        for o in range(1, reach + 1):
+            if (c, o, i) not in sent:
+                sent.add((c, o, i))
+                send_blocks[c, o, i].wait_send()
+
+    def send_piece(c, i):
+        place = order.index((c, i))
+        if place >= 2:
+            left(*order[place - 2])
+        rows = block_rows(pieces[c][i])
+        for o in range(1, reach + 1):
+            copy = pltpu.make_async_remote_copy(
+                whitened.at[c, rows], held.at[o - 1, c, rows],
+                block_send.at[o - 1, c, i], block_recv.at[o - 1, c, i],
+                device_id=at(o, 0), device_id_type=MESH,
+            )
+            copy.start()
+            send_blocks[c, o, i] = copy
+
+    def own_visit(c):
         mine = whitened[c]
         cross = cross_sums(mine, mine, own_select[0], width).astype(jnp.bfloat16)
         part = lag_terms(inverse[c], cross).reshape(groups, share, cols)
@@ -192,17 +183,9 @@
             total += target[k].astype(jnp.float32)
         out[:, place * cols : (place + 1) * cols] = (total * scale).astype(jnp.bfloat16)
 
-    early_out[...] = terms[reach].astype(jnp.bfloat16)
-    early = [(send_result(early_out, early_in, early_send, early_recv, 0, k), k) for k in range(1, groups)]
-
-    for o in range(1, reach + 1):
-        send_visits[o - 1].wait_recv()
-        held_select[o - 1] = selector(held_visits[o - 1], sets, width)
-
     back, late = {}, {}
-    for c in range(CHUNKS):
-        if c == CHUNKS - 1:
-            finish(reach, terms[reach, group], early, early_in)
+
+    def held_visits_of(c):
         for o in range(1, reach + 1):
             up, down = 0.0, 0.0
             for i, piece in enumerate(pieces[c]):
@@ -230,10 +213,60 @@
                 refs = [ref.at[o - 1] for ref in (late_out, late_in, late_send, late_recv)]
                 late[o] = [(send_result(*refs, 0, k), k) for k in range(1, groups)]
 
+    for i, piece in enumerate(pieces[0]):
+        if i == 0:
+            load_table[0].wait()
+        load_records[i].wait()
+        whitened[0, block_rows(piece)] = whiten(transform(records[block_rows(piece)], forward[0]))
+        if i == 0:
+            for later in range(1, CHUNKS):
+                load_table[later].start()
+            load_inverse.start()
+            pl.semaphore_wait(barrier, len(partners))
+        send_piece(0, i)
+    load_visits.wait()
+    for o in range(1, reach + 1):
+        copy = pltpu.make_async_remote_copy(
+            visits.at[reach - o], held_visits.at[o - 1], visit_send.at[o - 1], visit_recv.at[o - 1],
+            device_id=at(o, 0), device_id_type=MESH,
+        )
+        copy.start()
+        send_visits.append(copy)
+    for c in range(1, CHUNKS):
+        load_table[c].wait()
+        whitened[c] = whiten(transform(records[...], forward[c]))
+        if c == 1:
+            for o in range(reach + 1):
+                own_select[o] = selector(visits[reach + o], sets, width)
+            load_inverse.wait()
+        own_visit(c - 1)
+        if c < CHUNKS - 1:
+            for i in range(len(pieces[c])):
+                send_piece(c, i)
+    own_visit(CHUNKS - 1)
+
+    early_out[...] = terms[reach].astype(jnp.bfloat16)
+    early = [(send_result(early_out, early_in, early_send, early_recv, 0, k), k) for k in range(1, groups)]
+
+    for o in range(1, reach + 1):
+        send_visits[o - 1].wait_recv()
+        held_select[o - 1] = selector(held_visits[o - 1], sets, width)
+
+    for c in range(CHUNKS):
+        held_visits_of(c)
+        if c < CHUNKS - 1 and c < len(pieces[-1]):
+            send_piece(CHUNKS - 1, c)
+        if c == CHUNKS - 2:
+            for i in range(CHUNKS - 1, len(pieces[-1])):
+                send_piece(CHUNKS - 1, i)
+            finish(reach, terms[reach, group], early, early_in)
+
     for o in range(1, reach + 1):
         finish(reach - o, 0.0, back[o], back_in.at[o - 1])
         finish(reach + o, terms[reach + o, group], late[o], late_in.at[o - 1])
-    for copy in send_visits + list(send_blocks.values()) + send_results:
+    for piece in order:
+        left(*piece)
+    for copy in send_visits + send_results:
         copy.wait_send()
 
 

time: 24.3 us -> 26.1 us (1.074)
  Pallas kernels: 23.4 us -> 25.2 us
    pallas_call x1, Pallas kernels: 23.4 us -> 25.2 us  [local(): pl.pallas_call(functools.partial(kernel, (reach, days, segs, blocks, sets...]
where the time goes in v6:
time: 26.1 us; the launch traced here: 26 us
  Pallas kernels  25.2 us (97%)
  local copies, waits for them, and re-layouts  0.76 us (3%)
    pallas_call x1, Pallas kernels, local(): pl.pallas_call(functools.partial(kernel, (reach, days, segs, blocks, sets...  25.2 us
    reshape x1, local copies, waits for them, and re-layouts, local(): return result.reshape(share, visit_count, picks, width)  0.76 us

profile of v6, /device:TPU:0, one launch (start us, length us, event | category | flops | bytes accessed | tf_op | source)
XLA Modules:
  0.0 26.0 jit_solution(15269112302124989522)
XLA Ops:
  0.0 25.2 %correlate.1 = bf16[64,384]{1,0:T(8,128)(2,1)S(1)} custom-call(bf16[256,2048]{1,0:T(8,128)(2,1)} %bitcast.1, s32[3,2,64]{2,1,0:T(2,128)} %visits_hbm.1, bf16[4,1024,256]{2,1,0:T(8,128)(2,1)} %constant.4.clone.forward_hbm, bf16[4,256,256]{2,1,0:T(8,128)(2,1)} %constant.5.clone.inverse_hbm), custom_call_target="tpu_custom_call" | custom-call | flops 1275068416 | bytes 8388608 | tf_op jit(solution)/shard_map/correlate/pallas_call | solution.py:290
  25.2 0.8 %reshape.7 = bf16[64,3,2,64]{3,2,1,0:T(2,128)(2,1)} reshape(bf16[64,384]{1,0:T(8,128)(2,1)S(1)} %correlate.1) | data formatting | bytes 98304 | tf_op jit(solution)/shard_map/reshape | solution.py:322

commit v7 on v6

--- a/solution.py
+++ b/solution.py
@@ -113,7 +113,7 @@
     half = sets // 2
     halves = [(0, half), (half, sets - half)] if sets > 1 else [(0, sets)]
     parts = [(0, half), (half, sets - 1 - half), (sets - 1, 1)] if sets > 2 else halves
-    pieces = [halves if c == 0 else parts if c == CHUNKS - 1 else [(0, sets)] for c in range(CHUNKS)]
+    pieces = [parts if c == CHUNKS - 1 else halves for c in range(CHUNKS)]
 
     def block_rows(piece):
         return pl.ds(piece[0] * width, piece[1] * width)
@@ -136,19 +136,9 @@
     partners = [(o, k) for o in range(-reach, reach + 1) for k in range(groups) if (o, k) != (0, 0)]
     for o, k in partners:
         pl.semaphore_signal(barrier, inc=1, device_id=at(o, k), device_id_type=MESH)
-    order = [(c, i) for c in range(CHUNKS) for i in range(len(pieces[c]))]
-    send_visits, send_blocks, sent = [], {}, set()
-
-    def left(c, i):
-        for o in range(1, reach + 1):
-            if (c, o, i) not in sent:
-                sent.add((c, o, i))
-                send_blocks[c, o, i].wait_send()
+    send_visits, send_blocks = [], {}
 
     def send_piece(c, i):
-        place = order.index((c, i))
-        if place >= 2:
-            left(*order[place - 2])
         rows = block_rows(pieces[c][i])
         for o in range(1, reach + 1):
             copy = pltpu.make_async_remote_copy(
@@ -188,8 +178,10 @@
     def held_visits_of(c):
         for o in range(1, reach + 1):
             up, down = 0.0, 0.0
-            for i, piece in enumerate(pieces[c]):
-                send_blocks[c, o, i].wait_recv()
+            work = pieces[c] if c == CHUNKS - 1 else [(0, sets)]
+            for i, piece in enumerate(work):
+                for j in range(len(pieces[c])) if c < CHUNKS - 1 else [i]:
+                    send_blocks[c, o, j].wait_recv()
                 mine, theirs = whitened[c, block_rows(piece)], held[o - 1, c, block_rows(piece)]
                 part = (slice(0, piece[1] * cols), slice(0, piece[1] * width))
                 up += cross_sums(theirs, mine, held_select[o - 1][part], width)
@@ -234,16 +226,14 @@
         send_visits.append(copy)
     for c in range(1, CHUNKS):
         load_table[c].wait()
-        whitened[c] = whiten(transform(records[...], forward[c]))
-        if c == 1:
-            for o in range(reach + 1):
-                own_select[o] = selector(visits[reach + o], sets, width)
-            load_inverse.wait()
-        own_visit(c - 1)
-        if c < CHUNKS - 1:
-            for i in range(len(pieces[c])):
-                send_piece(c, i)
-    own_visit(CHUNKS - 1)
+        for i, piece in enumerate(pieces[c]):
+            whitened[c, block_rows(piece)] = whiten(transform(records[block_rows(piece)], forward[c]))
+            send_piece(c, i)
+    for o in range(reach + 1):
+        own_select[o] = selector(visits[reach + o], sets, width)
+    load_inverse.wait()
+    for c in range(CHUNKS):
+        own_visit(c)
 
     early_out[...] = terms[reach].astype(jnp.bfloat16)
     early = [(send_result(early_out, early_in, early_send, early_recv, 0, k), k) for k in range(1, groups)]
@@ -253,20 +243,14 @@
         held_select[o - 1] = selector(held_visits[o - 1], sets, width)
 
     for c in range(CHUNKS):
+        if c == CHUNKS - 1:
+            finish(reach, terms[reach, group], early, early_in)
         held_visits_of(c)
-        if c < CHUNKS - 1 and c < len(pieces[-1]):
-            send_piece(CHUNKS - 1, c)
-        if c == CHUNKS - 2:
-            for i in range(CHUNKS - 1, len(pieces[-1])):
-                send_piece(CHUNKS - 1, i)
-            finish(reach, terms[reach, group], early, early_in)
 
     for o in range(1, reach + 1):
         finish(reach - o, 0.0, back[o], back_in.at[o - 1])
         finish(reach + o, terms[reach + o, group], late[o], late_in.at[o - 1])
-    for piece in order:
-        left(*piece)
-    for copy in send_visits + send_results:
+    for copy in send_visits + list(send_blocks.values()) + send_results:
         copy.wait_send()
 
 

time: 26.1 us -> 24.3 us (0.931)
  Pallas kernels: 25.2 us -> 23.4 us
    pallas_call x1, Pallas kernels: 25.2 us -> 23.4 us  [local(): pl.pallas_call(functools.partial(kernel, (reach, days, segs, blocks, sets...]
where the time goes in v7:
time: 24.3 us; the launch traced here: 24.1 us
  Pallas kernels  23.4 us (96%)
  local copies, waits for them, and re-layouts  0.76 us (3%)
    pallas_call x1, Pallas kernels, local(): pl.pallas_call(functools.partial(kernel, (reach, days, segs, blocks, sets...  23.4 us
    reshape x1, local copies, waits for them, and re-layouts, local(): return result.reshape(share, visit_count, picks, width)  0.76 us

profile of v7, /device:TPU:0, one launch (start us, length us, event | category | flops | bytes accessed | tf_op | source)
XLA Modules:
  0.0 24.1 jit_solution(17633884511128938125)
XLA Ops:
  0.0 23.4 %correlate.1 = bf16[64,384]{1,0:T(8,128)(2,1)S(1)} custom-call(bf16[256,2048]{1,0:T(8,128)(2,1)} %bitcast.1, s32[3,2,64]{2,1,0:T(2,128)} %visits_hbm.1, bf16[4,1024,256]{2,1,0:T(8,128)(2,1)} %constant.4.clone.forward_hbm, bf16[4,256,256]{2,1,0:T(8,128)(2,1)} %constant.5.clone.inverse_hbm), custom_call_target="tpu_custom_call" | custom-call | flops 1275068416 | bytes 8388608 | tf_op jit(solution)/shard_map/correlate/pallas_call | solution.py:274
  23.4 0.8 %reshape.7 = bf16[64,3,2,64]{3,2,1,0:T(2,128)(2,1)} reshape(bf16[64,384]{1,0:T(8,128)(2,1)S(1)} %correlate.1) | data formatting | bytes 98304 | tf_op jit(solution)/shard_map/reshape | solution.py:306

commit v8 on v7

--- a/solution.py
+++ b/solution.py
@@ -184,13 +184,15 @@
                     send_blocks[c, o, j].wait_recv()
                 mine, theirs = whitened[c, block_rows(piece)], held[o - 1, c, block_rows(piece)]
                 part = (slice(0, piece[1] * cols), slice(0, piece[1] * width))
+                down += cross_sums(mine, theirs, own_select[o][part], width)
+                if c == CHUNKS - 1 and i == len(work) - 1:
+                    last = lag_terms(inverse[c], down.astype(jnp.bfloat16)).reshape(groups, share, cols)
+                    last += terms[reach + o]
+                    terms[reach + o] = last
+                    late_out[o - 1] = last.astype(jnp.bfloat16)
+                    refs = [ref.at[o - 1] for ref in (late_out, late_in, late_send, late_recv)]
+                    late[o] = [(send_result(*refs, 0, k), k) for k in range(1, groups)]
                 up += cross_sums(theirs, mine, held_select[o - 1][part], width)
-                if c == CHUNKS - 1 and i == len(pieces[c]) - 1:
-                    last = lag_terms(inverse[c], up.astype(jnp.bfloat16)).reshape(groups, share, cols)
-                    back_out[o - 1] = (terms[reach - o] + last).astype(jnp.bfloat16)
-                    refs = [ref.at[o - 1] for ref in (back_out, back_in, back_send, back_recv)]
-                    back[o] = [(send_result(*refs, -o, k), k) for k in range(groups)]
-                down += cross_sums(mine, theirs, own_select[o][part], width)
             if c < CHUNKS - 1:
                 both = jnp.concatenate([down, up], 0).astype(jnp.bfloat16)
                 both = lag_terms(inverse[c], both)
@@ -198,12 +200,10 @@
                     piece = piece.reshape(groups, share, cols)
                     terms[place] = piece if c == 0 else terms[place] + piece
             else:
-                last = lag_terms(inverse[c], down.astype(jnp.bfloat16)).reshape(groups, share, cols)
-                last += terms[reach + o]
-                terms[reach + o] = last
-                late_out[o - 1] = last.astype(jnp.bfloat16)
-                refs = [ref.at[o - 1] for ref in (late_out, late_in, late_send, late_recv)]
-                late[o] = [(send_result(*refs, 0, k), k) for k in range(1, groups)]
+                last = lag_terms(inverse[c], up.astype(jnp.bfloat16)).reshape(groups, share, cols)
+                back_out[o - 1] = (terms[reach - o] + last).astype(jnp.bfloat16)
+                refs = [ref.at[o - 1] for ref in (back_out, back_in, back_send, back_recv)]
+                back[o] = [(send_result(*refs, -o, k), k) for k in range(groups)]
 
     for i, piece in enumerate(pieces[0]):
         if i == 0:
@@ -248,8 +248,8 @@
         held_visits_of(c)
 
     for o in range(1, reach + 1):
+        finish(reach + o, terms[reach + o, group], late[o], late_in.at[o - 1])
         finish(reach - o, 0.0, back[o], back_in.at[o - 1])
-        finish(reach + o, terms[reach + o, group], late[o], late_in.at[o - 1])
     for copy in send_visits + list(send_blocks.values()) + send_results:
         copy.wait_send()
 

time: 24.3 us -> 24.3 us (level)
  no operation moved by 1% of the time
where the time goes in v8:
time: 24.3 us; the launch traced here: 24.2 us
  Pallas kernels  23.4 us (96%)
  local copies, waits for them, and re-layouts  0.76 us (3%)
    pallas_call x1, Pallas kernels, local(): pl.pallas_call(functools.partial(kernel, (reach, days, segs, blocks, sets...  23.4 us
    reshape x1, local copies, waits for them, and re-layouts, local(): return result.reshape(share, visit_count, picks, width)  0.76 us

profile of v8, /device:TPU:0, one launch (start us, length us, event | category | flops | bytes accessed | tf_op | source)
XLA Modules:
  0.0 24.2 jit_solution(10184907058436875708)
XLA Ops:
  0.0 23.4 %correlate.1 = bf16[64,384]{1,0:T(8,128)(2,1)S(1)} custom-call(bf16[256,2048]{1,0:T(8,128)(2,1)} %bitcast.1, s32[3,2,64]{2,1,0:T(2,128)} %visits_hbm.1, bf16[4,1024,256]{2,1,0:T(8,128)(2,1)} %constant.4.clone.forward_hbm, bf16[4,256,256]{2,1,0:T(8,128)(2,1)} %constant.5.clone.inverse_hbm), custom_call_target="tpu_custom_call" | custom-call | flops 1275068416 | bytes 8388608 | tf_op jit(solution)/shard_map/correlate/pallas_call | solution.py:274
  23.4 0.8 %reshape.7 = bf16[64,3,2,64]{3,2,1,0:T(2,128)(2,1)} reshape(bf16[64,384]{1,0:T(8,128)(2,1)S(1)} %correlate.1) | data formatting | bytes 98304 | tf_op jit(solution)/shard_map/reshape | solution.py:306

commit v9 on v7

--- a/solution.py
+++ b/solution.py
@@ -148,6 +148,13 @@
             )
             copy.start()
             send_blocks[c, o, i] = copy
+
+    def follow(c):
+        for place, copy in send_blocks.items():
+            if place[0] == c - 2:
+                copy.wait_send()
+        for i in range(len(pieces[c])):
+            send_piece(c, i)
 
     def own_visit(c):
         mine = whitened[c]
@@ -228,11 +235,15 @@
         load_table[c].wait()
         for i, piece in enumerate(pieces[c]):
             whitened[c, block_rows(piece)] = whiten(transform(records[block_rows(piece)], forward[c]))
-            send_piece(c, i)
+            if c == 1:
+                send_piece(c, i)
     for o in range(reach + 1):
         own_select[o] = selector(visits[reach + o], sets, width)
     load_inverse.wait()
-    for c in range(CHUNKS):
+    own_visit(0)
+    own_visit(1)
+    follow(2)
+    for c in range(2, CHUNKS):
         own_visit(c)
 
     early_out[...] = terms[reach].astype(jnp.bfloat16)
@@ -246,11 +257,13 @@
         if c == CHUNKS - 1:
             finish(reach, terms[reach, group], early, early_in)
         held_visits_of(c)
+        if c + 3 < CHUNKS:
+            follow(c + 3)
 
     for o in range(1, reach + 1):
         finish(reach - o, 0.0, back[o], back_in.at[o - 1])
         finish(reach + o, terms[reach + o, group], late[o], late_in.at[o - 1])
-    for copy in send_visits + list(send_blocks.values()) + send_results:
+    for copy in send_visits + [send_blocks[p] for p in send_blocks if p[0] >= CHUNKS - 2] + send_results:
         copy.wait_send()
 
 

time: 24.3 us -> 24.3 us (level)
  no operation moved by 1% of the time
where the time goes in v9:
time: 24.3 us; the launch traced here: 24.1 us
  Pallas kernels  23.4 us (96%)
  local copies, waits for them, and re-layouts  0.76 us (3%)
    pallas_call x1, Pallas kernels, local(): pl.pallas_call(functools.partial(kernel, (reach, days, segs, blocks, sets...  23.4 us
    reshape x1, local copies, waits for them, and re-layouts, local(): return result.reshape(share, visit_count, picks, width)  0.76 us

profile of v9, /device:TPU:0, one launch (start us, length us, event | category | flops | bytes accessed | tf_op | source)
XLA Modules:
  0.0 24.1 jit_solution(8982847853619494838)
XLA Ops:
  0.0 23.4 %correlate.1 = bf16[64,384]{1,0:T(8,128)(2,1)S(1)} custom-call(bf16[256,2048]{1,0:T(8,128)(2,1)} %bitcast.1, s32[3,2,64]{2,1,0:T(2,128)} %visits_hbm.1, bf16[4,1024,256]{2,1,0:T(8,128)(2,1)} %constant.4.clone.forward_hbm, bf16[4,256,256]{2,1,0:T(8,128)(2,1)} %constant.5.clone.inverse_hbm), custom_call_target="tpu_custom_call" | custom-call | flops 1275068416 | bytes 8388608 | tf_op jit(solution)/shard_map/correlate/pallas_call | solution.py:287
  23.4 0.8 %reshape.7 = bf16[64,3,2,64]{3,2,1,0:T(2,128)(2,1)} reshape(bf16[64,384]{1,0:T(8,128)(2,1)S(1)} %correlate.1) | data formatting | bytes 98304 | tf_op jit(solution)/shard_map/reshape | solution.py:319

commit v10 on v9

--- a/solution.py
+++ b/solution.py
@@ -127,15 +127,15 @@
     load_table = [
         pltpu.make_async_copy(forward_hbm.at[c], forward.at[c], table_sem.at[c]) for c in range(CHUNKS)
     ]
+    barrier = pltpu.get_barrier_semaphore()
+    partners = [(o, k) for o in range(-reach, reach + 1) for k in range(groups) if (o, k) != (0, 0)]
+    for o, k in sorted(partners, key=lambda p: p[1] != 0):
+        pl.semaphore_signal(barrier, inc=1, device_id=at(o, k), device_id_type=MESH)
     load_table[0].start()
     for copy in load_records:
         copy.start()
     load_visits.start()
 
-    barrier = pltpu.get_barrier_semaphore()
-    partners = [(o, k) for o in range(-reach, reach + 1) for k in range(groups) if (o, k) != (0, 0)]
-    for o, k in partners:
-        pl.semaphore_signal(barrier, inc=1, device_id=at(o, k), device_id_type=MESH)
     send_visits, send_blocks = [], {}
 
     def send_piece(c, i):

time: 24.3 us -> 24.2 us (level)
  no operation moved by 1% of the time
where the time goes in v10:
time: 24.2 us; the launch traced here: 24.1 us
  Pallas kernels  23.3 us (96%)
  local copies, waits for them, and re-layouts  0.76 us (3%)
    pallas_call x1, Pallas kernels, local(): pl.pallas_call(functools.partial(kernel, (reach, days, segs, blocks, sets...  23.3 us
    reshape x1, local copies, waits for them, and re-layouts, local(): return result.reshape(share, visit_count, picks, width)  0.76 us

profile of v10, /device:TPU:0, one launch (start us, length us, event | category | flops | bytes accessed | tf_op | source)
XLA Modules:
  0.0 24.1 jit_solution(3536429356806964062)
XLA Ops:
  0.0 23.3 %correlate.1 = bf16[64,384]{1,0:T(8,128)(2,1)S(1)} custom-call(bf16[256,2048]{1,0:T(8,128)(2,1)} %bitcast.1, s32[3,2,64]{2,1,0:T(2,128)} %visits_hbm.1, bf16[4,1024,256]{2,1,0:T(8,128)(2,1)} %constant.4.clone.forward_hbm, bf16[4,256,256]{2,1,0:T(8,128)(2,1)} %constant.5.clone.inverse_hbm), custom_call_target="tpu_custom_call" | custom-call | flops 1275068416 | bytes 8388608 | tf_op jit(solution)/shard_map/correlate/pallas_call | solution.py:287
  23.3 0.8 %reshape.7 = bf16[64,3,2,64]{3,2,1,0:T(2,128)(2,1)} reshape(bf16[64,384]{1,0:T(8,128)(2,1)S(1)} %correlate.1) | data formatting | bytes 98304 | tf_op jit(solution)/shard_map/reshape | solution.py:319
